TPU v7x, 512 devices: a whole 4x8x8 slice. The times are simulated.
512 devices in a mesh: lon: 16 (over z, core), lat: 32 (over y, x).
Axes of the slice: x: 4, y: 8, z: 8, core: 2. Of those that a mesh axis runs over, the one named last changes fastest.
Arguments:
- increment: float32 [2, 64, 768, 2048], P(None, None, 'lat', 'lon'), may hold values from -6 to 6
- eastward_rate: float32 [2, 64, 768], P(None, None, 'lat'), as said below
- eastward_spike: float32 [768, 2048], P('lat', 'lon'), as said below
- northward_rate: float32 [2, 64, 768], replicated, as said below
- vertical: float32 [2, 64, 64], replicated, may hold values from -0.75 to 0.75
Outputs:
- correlated: float32 [2, 64, 768, 2048], P(None, None, 'lat', 'lon')
Inputs may be any that keep to these rules, and one draw needn't show every extreme that they name: `eastward_rate`: every entry is positive and below 1. `eastward_spike`: every entry is positive and at most 1. `northward_rate`: every entry is positive and below 1.
All inputs are finite; a program needn't handle non-finite values.
Results may differ from a plain program's by a relative error of at most 0.0003.
Values sent between devices are 32-bit elements; how exact they have to be, the bound alone decides.
A program may use at most 64 MiB of HBM per device.

v0:
```python
import jax
import jax.numpy as jnp
from jax import lax
from jax.sharding import PartitionSpec as P


def carried_in(x, axis, combine, identity):
    length, mine = (lax.axis_size(axis), lax.axis_index(axis))
    everything = jax.tree.map(lambda part: lax.all_gather(part, axis), x)
    start = jax.tree.map(
        lambda part, zero: jnp.broadcast_to(jnp.asarray(zero, part.dtype), part.shape), x, identity
    )

    def lap(k, before):
        at = length - 1 - k
        reached = at > mine
        new = combine(before, jax.tree.map(lambda part: part[at], everything))
        return jax.tree.map(lambda a, b: jnp.where(reached, a, b), new, before)

    return lax.fori_loop(0, length, lap, start)


def from_root(block, axis, source):
    block = jnp.where(lax.axis_index(axis) == source, block, jnp.zeros_like(block))
    return lax.psum(block, axis)


def compose(earlier, following):
    return (following[0] * earlier[0], following[1] + following[0] * earlier[1])


def matmul_last(values, matrix):
    flat = values.reshape((-1, values.shape[-1]))
    result = jnp.dot(
        flat, matrix, precision=lax.Precision.HIGHEST, preferred_element_type=jnp.float32
    )
    return result.reshape(values.shape[:-1] + (matrix.shape[1],))


def row_filter(rates):
    length = rates.shape[-1]
    totals = jnp.cumsum(jnp.log(rates), axis=-1)
    upper = lax.broadcasted_iota(jnp.int32, (length, length), 0)
    lower = lax.broadcasted_iota(jnp.int32, (length, length), 1)
    keeping = lower <= upper
    spread = totals[..., :, None] - totals[..., None, :]
    weights = jnp.where(keeping, jnp.exp(jnp.where(keeping, spread, -60.0)), 0.0)
    return (weights, jnp.exp(totals))


def shards(increment, eastward_rate, eastward_spike, northward_rate, vertical):
    lon_cols = increment.shape[3]
    decay_factors = eastward_rate[:, :, :, None] * eastward_spike[None, None, :, :]
    row_index = lax.broadcasted_iota(jnp.int32, (lon_cols, lon_cols), 0)
    col_index = lax.broadcasted_iota(jnp.int32, (lon_cols, lon_cols), 1)
    before_mat = (row_index < col_index).astype(jnp.float32)
    suffix_mat = (row_index >= col_index).astype(jnp.float32)
    log_decay = jnp.log(decay_factors)
    prefix_log = matmul_last(log_decay, before_mat)
    total_log = jnp.sum(log_decay, axis=3)
    suffix_sums = matmul_last(jnp.exp(prefix_log) * increment, suffix_mat)
    local_part = jnp.exp(-prefix_log) * suffix_sums
    factor = jnp.exp(total_log[:, :, :, None] - prefix_log)
    block_factor = jnp.exp(total_log)
    block_local = local_part[:, :, :, 0]
    identity_map = (jnp.ones_like(block_factor), jnp.zeros_like(block_local))
    after_factor, after_local = carried_in(
        (block_factor, block_local), "lon", compose, identity_map
    )
    whole_factor, whole_local = compose((after_factor, after_local), (block_factor, block_local))
    shared = from_root(jnp.stack([whole_factor, whole_local]), "lon", 0)
    loop_factor = shared[0]
    loop_local = shared[1]
    wrapped = loop_local / (1.0 - loop_factor)
    incoming = after_local + after_factor * wrapped
    eastward_output = jnp.sqrt(1.0 - decay_factors * decay_factors) * (
        local_part + factor * incoming[:, :, :, None]
    )
    columns = lax.all_to_all(eastward_output, "lat", split_axis=1, concat_axis=2, tiled=True)
    levels_here = columns.shape[1]
    first_level = lax.axis_index("lat") * levels_here
    row_rates = lax.dynamic_slice_in_dim(northward_rate, first_level, levels_here, 1)
    weights, growth = row_filter(row_rates)
    filtered = jnp.einsum("vljk,vlki->vlji", weights, columns, precision=lax.Precision.HIGHEST)
    scaled = jnp.sqrt(1.0 - row_rates * row_rates)[:, :, :, None] * filtered
    meridional_out = lax.all_to_all(scaled, "lat", split_axis=2, concat_axis=1, tiled=True)
    return jnp.einsum("vlk,vlab->vkab", vertical, meridional_out, precision=lax.Precision.HIGHEST)


def solution(mesh):
    return jax.shard_map(
        shards,
        mesh=mesh,
        in_specs=(P(None, None, "lat", "lon"), P(None, None, "lat"), P("lat", "lon"), P(), P()),
        out_specs=P(None, None, "lat", "lon"),
        check_vma=False,
    )
```

profile of v0, /device:TPU:192, one launch (start us, length us, event | category | flops | bytes accessed | tf_op | source)
XLA Modules:
  0.0 217.6 jit_solution(4784289971304212418)
XLA Ops:
  0.0 0.9 copy.57
  0.9 1.7 fusion.12
  2.6 0.9 fusion.11
  3.5 2.4 %exponential_multiply_fusion = f32[2,64,24,128]{3,2,1,0:T(8,128)S(1)} fusion(f32[2,64,24,128]{3,2,1,0:T(8,128)S(1)} %fusion.12, f32[2,64,24,128]{3,2,1,0:T(8,128)} %param.7), kind=kOutput, calls=%fused_computation.25 | convolution fusion | flops 605175808 | bytes 4718592 | tf_op jit(solution)/shard_map/dot_general | solution.py:34
  6.5 19.0 %all-gather.1 = f32[32,64,24,1]{1,2,3,0:T(8,128)} all-gather(f32[2,64,24,1]{1,2,3,0:T(8,128)S(1)} %copy.59), channel_id=3, replica_groups=mesh['lon'=16,'lat'=32] {'lon'}, dimensions={0}, use_global_device_ids=true | all-gather | bytes 208896 | tf_op jit(solution)/shard_map/all_gather | solution.py:9
  25.6 19.0 %all-gather = f32[32,64,24]{1,2,0:T(8,128)} all-gather(f32[2,64,24]{1,2,0:T(8,128)S(1)} %exp.29), channel_id=2, replica_groups=mesh['lon'=16,'lat'=32] {'lon'}, dimensions={0}, use_global_device_ids=true | all-gather | bytes 208896 | tf_op jit(solution)/shard_map/all_gather | solution.py:9
  44.6 12.8 %while.18 = (s32[]{:T(128)}, f32[2,64,24]{1,2,0:T(8,128)S(1)}, f32[2,64,24]{1,2,0:T(8,128)S(1)}, s32[]{:T(128)}, f32[16,2,64,24]{2,3,1,0:T(8,128)}, /*index=5*/f...) while((s32[]{:T(128)}, f32[2,64,24]{1,2,0:T(8,128)S(1)}, ...), condition=%wide.region_4.5_spmd.clone, body=%wide.region_3.4_spmd.clone.sunk | while | flops 21512 | bytes 73899 | solution.py:20
  45.4 0.8 fusion.41
  46.2 0.8 fusion.41
  52.6 0.8 fusion.41
  53.4 0.8 fusion.41
  57.4 44.1 %psum.7 = f32[2,2,64,24]{2,3,1,0:T(8,128)S(1)} all-reduce(f32[2,2,64,24]{2,3,1,0:T(8,128)S(1)} %maximum_select_fusion), channel_id=1, replica_groups=mesh['lon'=16,'lat'=32] {'lon'}, use_global_device_ids=true, to_apply=%region_5.6 | all-reduce | flops 6144 | bytes 49152 | tf_op jit(solution)/shard_map/psum | solution.py:25
  101.6 1.5 fusion.15
  103.2 1.3 copy.62
  104.5 9.9 %all-to-all-start = ((f32[2,64,24,128]{3,2,0,1:T(8,128)}), f32[2,64,24,128]{3,2,0,1:T(8,128)S(1)}, u32[]{:S(2)}, u32[]{:S(2)}) async-start(f32[2,64,24,128]{3,2,0,1:T(8,128)} %copy.62), calls=%async_computation | async-start | bytes 3145728 | tf_op jit(solution)/shard_map/all_to_all | solution.py:79
  114.4 0.8 subtract_sqrt_fusion
  115.3 1.2 reduce-window.6
  117.3 37.2 %all-to-all-done = f32[2,64,24,128]{3,2,0,1:T(8,128)S(1)} async-done(((f32[2,64,24,128]{3,2,0,1:T(8,128)}), f32[2,64,24,128]{3,2,0,1:T(8,128)S(1)}, u32[]{:S(2)}, u32[]{:S(2)}) %all-to-all-start) | async-done | bytes 1572896 | tf_op jit(solution)/shard_map/all_to_all | solution.py:79
  154.6 10.2 %fusion.21 = f32[2,2,768,128]{3,2,1,0:T(8,128)S(1)} fusion(f32[2,2,768,128]{3,2,1,0:T(8,128)S(1)} %bitcast.62, f32[2,2,768]{2,1,0:T(2,128)S(1)} %reduce_window_sum.23, pred[768,768]{1,0:T(8,128)(4,1)S(1)} %iota_compare_fusion, f32[2,2,768]{2,1,0:T(2,128)S(1)} %get-tuple-element.203), kind=kOutput, calls=%fused_computation.27 | convolution fusion | flops 3631349760 | bytes 3760128 | tf_op jit(solution)/shard_map/vljk,vlki->vlji/dot_general | solution.py:84
  164.8 1.4 copy.64
  166.3 46.9 %all_to_all.36 = f32[2,2,768,128]{3,1,0,2:T(2,128)S(1)} all-to-all(f32[2,2,768,128]{3,1,0,2:T(2,128)S(1)} %copy.64), channel_id=1, replica_groups=mesh['lon'=16,'lat'=32] {'lat'}, dimensions={2} | all-to-all | bytes 3145728 | tf_op jit(solution)/shard_map/all_to_all | solution.py:86
  213.1 0.9 copy.65
  214.0 1.5 convolution_bitcast_fusion
  215.5 2.1 copy.67
  (32 shorter events, 11.0 us)
Async XLA Ops:
  0.0 214.0 %copy-start = (f32[2,64,64]{2,1,0:T(8,128)S(1)}, f32[2,64,64]{2,1,0:T(8,128)}, u32[]{:S(2)}) copy-start(f32[2,64,64]{2,1,0:T(8,128)} %param.11) | copy-start | bytes 98308
  0.0 2.6 %copy-start.1 = (f32[24,128]{1,0:T(8,128)S(1)}, f32[24,128]{1,0:T(8,128)}, u32[]{:S(2)}) copy-start(f32[24,128]{1,0:T(8,128)} %param.9) | copy-start | bytes 36868
  104.5 50.1 %all-to-all-start = ((f32[2,64,24,128]{3,2,0,1:T(8,128)}), f32[2,64,24,128]{3,2,0,1:T(8,128)S(1)}, u32[]{:S(2)}, u32[]{:S(2)}) async-start(f32[2,64,24,128]{3,2,0,1:T(8,128)} %copy.62), calls=%async_computation | async-start | bytes 3145728 | tf_op jit(solution)/shard_map/all_to_all | solution.py:79
where the time goes:
time: 219 us; the launch traced here: 218 us
  blocking collectives  129 us (59%)
  waiting for transfers between devices  37.2 us (17%)
  other arithmetic  17.5 us (8%)
  matrix products  15.8 us (7%)
  starting transfers between devices  9.95 us (5%)
  local copies, waits for them, and re-layouts  7.5 us (3%)
    all_to_all x1, blocking collectives, shards(): lax.all_to_all(scaled, 'lat', split_axis=2, concat_axis=1, tiled=True)  46.9 us
    psum x1, blocking collectives, from_root(): return lax.psum(block, axis)  44.1 us
    all_gather x2, blocking collectives, carried_in(): everything = jax.tree.map(lambda part: lax.all_gather(part, axis), x)  37.9 us
    all_to_all x1, waiting for transfers between devices, shards(): lax.all_to_all(eastward_output, 'lat', split_axis=1, concat_axis=2, tiled...  37.2 us
    select_n x16, other arithmetic, lap(): return jax.tree.map(lambda a, b: jnp.where(reached, a, b), new, before)  12.4 us
    dot_general x1, matrix products, shards(): jnp.einsum('vljk,vlki->vlji', weights, columns, precision=lax.Precision.H...  10.2 us
    all_to_all x1, starting transfers between devices, shards(): lax.all_to_all(eastward_output, 'lat', split_axis=1, concat_axis=2, tiled...  9.95 us
  transfers between devices with their start and end apart: 1, of which 1 were waited for; matrix products, arithmetic and copies ran while one was open for 1% of the time, Pallas kernels for 0%

commit v1 on v0

--- a/solution.py
+++ b/solution.py
@@ -83,7 +83,10 @@
     weights, growth = row_filter(row_rates)
     filtered = jnp.einsum("vljk,vlki->vlji", weights, columns, precision=lax.Precision.HIGHEST)
     scaled = jnp.sqrt(1.0 - row_rates * row_rates)[:, :, :, None] * filtered
-    meridional_out = lax.all_to_all(scaled, "lat", split_axis=2, concat_axis=1, tiled=True)
+    meridional_out = jnp.concatenate(
+        lax.all_to_all(jnp.stack(jnp.split(scaled, lax.axis_size("lat"), axis=2)), "lat", 0, 0),
+        axis=1,
+    )
     return jnp.einsum("vlk,vlab->vkab", vertical, meridional_out, precision=lax.Precision.HIGHEST)
 
 

time: 219 us -> 218 us (level)
  the two profiles are of different devices: /device:TPU:192 before, /device:TPU:8 now
where the time goes in v1:
time: 218 us; the launch traced here: 217 us
  blocking collectives  133 us (61%)
  waiting for transfers between devices  31.9 us (15%)
  other arithmetic  18.2 us (8%)
  matrix products  15.9 us (7%)
  starting transfers between devices  10.2 us (5%)
  local copies, waits for them, and re-layouts  6.46 us (3%)
    psum x1, blocking collectives, from_root(): return lax.psum(block, axis)  47.3 us
    all_to_all x1, blocking collectives, shards(): lax.all_to_all(jnp.stack(jnp.split(scaled, lax.axis_size('lat'), axis=2))...  43.2 us
    all_gather x2, blocking collectives, carried_in(): everything = jax.tree.map(lambda part: lax.all_gather(part, axis), x)  42.6 us
    all_to_all x1, waiting for transfers between devices, shards(): lax.all_to_all(eastward_output, 'lat', split_axis=1, concat_axis=2, tiled...  31.9 us
    select_n x16, other arithmetic, lap(): return jax.tree.map(lambda a, b: jnp.where(reached, a, b), new, before)  12.4 us
    all_to_all x1, starting transfers between devices, shards(): lax.all_to_all(eastward_output, 'lat', split_axis=1, concat_axis=2, tiled...  10.2 us
    dot_general x1, matrix products, shards(): jnp.einsum('vljk,vlki->vlji', weights, columns, precision=lax.Precision.H...  10 us
  transfers between devices with their start and end apart: 1, of which 1 were waited for; matrix products, arithmetic and copies ran while one was open for 2% of the time, Pallas kernels for 0%

profile of v1, /device:TPU:8, one launch (start us, length us, event | category | flops | bytes accessed | tf_op | source)
XLA Modules:
  0.0 216.6 jit_solution(8549013409714084407)
XLA Ops:
  0.0 0.9 copy.57
  0.9 1.7 fusion.12
  2.6 0.9 fusion.11
  3.5 2.4 %exponential_multiply_fusion = f32[2,64,24,128]{3,2,1,0:T(8,128)S(1)} fusion(f32[2,64,24,128]{3,2,1,0:T(8,128)S(1)} %fusion.12, f32[2,64,24,128]{3,2,1,0:T(8,128)} %param.7), kind=kOutput, calls=%fused_computation.27 | convolution fusion | flops 605175808 | bytes 4718592 | tf_op jit(solution)/shard_map/dot_general | solution.py:34
  6.5 25.6 %all-gather.1 = f32[32,64,24,1]{1,2,3,0:T(8,128)} all-gather(f32[2,64,24,1]{1,2,3,0:T(8,128)S(1)} %copy.59), channel_id=3, replica_groups=mesh['lon'=16,'lat'=32] {'lon'}, dimensions={0}, use_global_device_ids=true | all-gather | bytes 208896 | tf_op jit(solution)/shard_map/all_gather | solution.py:9
  32.2 16.9 %all-gather = f32[32,64,24]{1,2,0:T(8,128)} all-gather(f32[2,64,24]{1,2,0:T(8,128)S(1)} %exp.29), channel_id=2, replica_groups=mesh['lon'=16,'lat'=32] {'lon'}, dimensions={0}, use_global_device_ids=true | all-gather | bytes 208896 | tf_op jit(solution)/shard_map/all_gather | solution.py:9
  49.2 12.8 %while.18 = (s32[]{:T(128)}, f32[2,64,24]{1,2,0:T(8,128)S(1)}, f32[2,64,24]{1,2,0:T(8,128)S(1)}, s32[]{:T(128)}, f32[16,2,64,24]{2,3,1,0:T(8,128)}, /*index=5*/f...) while((s32[]{:T(128)}, f32[2,64,24]{1,2,0:T(8,128)S(1)}, ...), condition=%wide.region_4.5_spmd.clone, body=%wide.region_3.4_spmd.clone.sunk | while | flops 21512 | bytes 73899 | solution.py:20
  50.8 0.8 fusion.45
  51.6 0.8 fusion.45
  58.8 0.8 fusion.45
  59.6 0.8 fusion.45
  62.0 47.3 %psum.7 = f32[2,2,64,24]{2,3,1,0:T(8,128)S(1)} all-reduce(f32[2,2,64,24]{2,3,1,0:T(8,128)S(1)} %maximum_select_fusion), channel_id=1, replica_groups=mesh['lon'=16,'lat'=32] {'lon'}, use_global_device_ids=true, to_apply=%region_5.6 | all-reduce | flops 6144 | bytes 49152 | tf_op jit(solution)/shard_map/psum | solution.py:25
  109.4 1.5 fusion.15
  111.0 1.3 copy.62
  112.2 10.2 %all-to-all-start = ((f32[2,64,24,128]{3,2,0,1:T(8,128)}), f32[2,64,24,128]{3,2,0,1:T(8,128)S(1)}, u32[]{:S(2)}, u32[]{:S(2)}) async-start(f32[2,64,24,128]{3,2,0,1:T(8,128)} %copy.62), calls=%async_computation | async-start | bytes 3145728 | tf_op jit(solution)/shard_map/all_to_all | solution.py:79
  122.4 0.8 subtract_sqrt_fusion
  123.3 1.2 reduce-window.6
  125.0 1.0 iota_compare_fusion
  126.0 31.9 %all-to-all-done = f32[2,64,24,128]{3,2,0,1:T(8,128)S(1)} async-done(((f32[2,64,24,128]{3,2,0,1:T(8,128)}), f32[2,64,24,128]{3,2,0,1:T(8,128)S(1)}, u32[]{:S(2)}, u32[]{:S(2)}) %all-to-all-start) | async-done | bytes 1572896 | tf_op jit(solution)/shard_map/all_to_all | solution.py:79
  158.1 1.0 copy-done.1
  159.0 10.0 %fusion.26 = f32[2,2,768,128]{3,2,1,0:T(8,128)S(1)} fusion(f32[2,2,768,128]{3,2,1,0:T(8,128)S(1)} %bitcast.187, f32[2,2,768]{2,1,0:T(2,128)S(1)} %reduce_window_sum.23, pred[768,768]{1,0:T(8,128)(4,1)S(1)} %copy-done.1, f32[2,2,768]{2,1,0:T(2,128)S(1)} %get-tuple-element.203), kind=kOutput, calls=%fused_computation.29 | convolution fusion | flops 3631349760 | bytes 3760128 | tf_op jit(solution)/shard_map/vljk,vlki->vlji/dot_general | solution.py:84
  169.5 43.2 %all_to_all.23 = f32[32,2,2,24,128]{4,3,2,1,0:T(8,128)S(1)} all-to-all(f32[32,2,2,24,128]{4,3,2,1,0:T(8,128)S(1)} %constant_dynamic-update-slice_fusion), channel_id=1, replica_groups=mesh['lon'=16,'lat'=32] {'lat'}, dimensions={0} | all-to-all | bytes 3145728 | tf_op jit(solution)/shard_map/all_to_all | solution.py:87
  212.8 1.7 fusion.21
  214.5 2.1 copy.67
  (65 shorter events, 11.1 us)
Async XLA Ops:
  0.0 212.8 %copy-start = (f32[2,64,64]{2,1,0:T(8,128)S(1)}, f32[2,64,64]{2,1,0:T(8,128)}, u32[]{:S(2)}) copy-start(f32[2,64,64]{2,1,0:T(8,128)} %param.11) | copy-start | bytes 98308
  0.0 2.6 %copy-start.2 = (f32[24,128]{1,0:T(8,128)S(1)}, f32[24,128]{1,0:T(8,128)}, u32[]{:S(2)}) copy-start(f32[24,128]{1,0:T(8,128)} %param.9) | copy-start | bytes 36868
  112.2 45.7 %all-to-all-start = ((f32[2,64,24,128]{3,2,0,1:T(8,128)}), f32[2,64,24,128]{3,2,0,1:T(8,128)S(1)}, u32[]{:S(2)}, u32[]{:S(2)}) async-start(f32[2,64,24,128]{3,2,0,1:T(8,128)} %copy.62), calls=%async_computation | async-start | bytes 3145728 | tf_op jit(solution)/shard_map/all_to_all | solution.py:79
  158.0 1.1 copy-start.1

commit v2 on v0

--- a/solution.py
+++ b/solution.py
@@ -22,7 +22,7 @@
 
 def from_root(block, axis, source):
     block = jnp.where(lax.axis_index(axis) == source, block, jnp.zeros_like(block))
-    return lax.psum(block, axis)
+    return jnp.sum(lax.all_gather(block, axis), axis=0)
 
 
 def compose(earlier, following):

time: 219 us -> 198 us (0.904)
  the two profiles are of different devices: /device:TPU:192 before, /device:TPU:8 now
where the time goes in v2:
time: 198 us; the launch traced here: 196 us
  blocking collectives  107 us (54%)
  waiting for transfers between devices  36 us (18%)
  other arithmetic  18.7 us (9%)
  matrix products  15.8 us (8%)
  starting transfers between devices  10.2 us (5%)
  local copies, waits for them, and re-layouts  7.5 us (4%)
    all_to_all x1, blocking collectives, shards(): lax.all_to_all(scaled, 'lat', split_axis=2, concat_axis=1, tiled=True)  45.4 us
    all_gather x2, blocking collectives, carried_in(): everything = jax.tree.map(lambda part: lax.all_gather(part, axis), x)  42.6 us
    all_to_all x1, waiting for transfers between devices, shards(): lax.all_to_all(eastward_output, 'lat', split_axis=1, concat_axis=2, tiled...  36 us
    all_gather x1, blocking collectives, from_root(): return jnp.sum(lax.all_gather(block, axis), axis=0)  19.4 us
    select_n x16, other arithmetic, lap(): return jax.tree.map(lambda a, b: jnp.where(reached, a, b), new, before)  12.4 us
    all_to_all x1, starting transfers between devices, shards(): lax.all_to_all(eastward_output, 'lat', split_axis=1, concat_axis=2, tiled...  10.2 us
    dot_general x1, matrix products, shards(): jnp.einsum('vljk,vlki->vlji', weights, columns, precision=lax.Precision.H...  10.2 us
    dot_general x2, matrix products, matmul_last(): jnp.dot(flat, matrix, precision=lax.Precision.HIGHEST, preferred_element_...  4.16 us
  transfers between devices with their start and end apart: 1, of which 1 were waited for; matrix products, arithmetic and copies ran while one was open for 1% of the time, Pallas kernels for 0%

profile of v2, /device:TPU:8, one launch (start us, length us, event | category | flops | bytes accessed | tf_op | source)
XLA Modules:
  0.0 196.2 jit_solution(13924528311815205546)
XLA Ops:
  0.0 0.9 copy.56
  0.9 1.7 fusion.12
  2.6 0.9 fusion.11
  3.5 2.4 %exponential_multiply_fusion = f32[2,64,24,128]{3,2,1,0:T(8,128)S(1)} fusion(f32[2,64,24,128]{3,2,1,0:T(8,128)S(1)} %fusion.12, f32[2,64,24,128]{3,2,1,0:T(8,128)} %param.7), kind=kOutput, calls=%fused_computation.25 | convolution fusion | flops 605175808 | bytes 4718592 | tf_op jit(solution)/shard_map/dot_general | solution.py:34
  6.5 25.6 %all-gather.1 = f32[32,64,24,1]{1,2,3,0:T(8,128)} all-gather(f32[2,64,24,1]{1,2,3,0:T(8,128)S(1)} %copy.58), channel_id=3, replica_groups=mesh['lon'=16,'lat'=32] {'lon'}, dimensions={0}, use_global_device_ids=true | all-gather | bytes 208896 | tf_op jit(solution)/shard_map/all_gather | solution.py:9
  32.2 16.9 %all-gather = f32[32,64,24]{1,2,0:T(8,128)} all-gather(f32[2,64,24]{1,2,0:T(8,128)S(1)} %exp.29), channel_id=2, replica_groups=mesh['lon'=16,'lat'=32] {'lon'}, dimensions={0}, use_global_device_ids=true | all-gather | bytes 208896 | tf_op jit(solution)/shard_map/all_gather | solution.py:9
  49.2 12.8 %while.18 = (s32[]{:T(128)}, f32[2,64,24]{1,2,0:T(8,128)S(1)}, f32[2,64,24]{1,2,0:T(8,128)S(1)}, s32[]{:T(128)}, f32[16,2,64,24]{2,3,1,0:T(8,128)}, /*index=5*/f...) while((s32[]{:T(128)}, f32[2,64,24]{1,2,0:T(8,128)S(1)}, ...), condition=%wide.region_4.5_spmd.clone, body=%wide.region_3.4_spmd.clone.sunk | while | flops 21512 | bytes 73899 | solution.py:20
  50.8 0.8 fusion.41
  51.6 0.8 fusion.41
  58.8 0.8 fusion.41
  62.0 19.4 %all_gather.13 = f32[16,2,2,64,24]{3,4,2,1,0:T(8,128)} all-gather(f32[1,2,2,64,24]{3,4,2,1,0:T(8,128)S(1)} %maximum_select_fusion), channel_id=1, replica_groups=mesh['lon'=16,'lat'=32] {'lon'}, dimensions={0}, use_global_device_ids=true | all-gather | bytes 417792 | tf_op jit(solution)/shard_map/all_gather | solution.py:25
  81.4 1.2 reduce_sum.19
  82.7 1.5 fusion.15
  84.2 1.3 copy.61
  85.5 10.2 %all-to-all-start = ((f32[2,64,24,128]{3,2,0,1:T(8,128)}), f32[2,64,24,128]{3,2,0,1:T(8,128)S(1)}, u32[]{:S(2)}, u32[]{:S(2)}) async-start(f32[2,64,24,128]{3,2,0,1:T(8,128)} %copy.61), calls=%async_computation | async-start | bytes 3145728 | tf_op jit(solution)/shard_map/all_to_all | solution.py:79
  95.7 0.8 subtract_sqrt_fusion
  96.5 1.2 reduce-window.6
  98.5 36.0 %all-to-all-done = f32[2,64,24,128]{3,2,0,1:T(8,128)S(1)} async-done(((f32[2,64,24,128]{3,2,0,1:T(8,128)}), f32[2,64,24,128]{3,2,0,1:T(8,128)S(1)}, u32[]{:S(2)}, u32[]{:S(2)}) %all-to-all-start) | async-done | bytes 1572896 | tf_op jit(solution)/shard_map/all_to_all | solution.py:79
  134.7 10.2 %fusion.21 = f32[2,2,768,128]{3,2,1,0:T(8,128)S(1)} fusion(f32[2,2,768,128]{3,2,1,0:T(8,128)S(1)} %bitcast.62, f32[2,2,768]{2,1,0:T(2,128)S(1)} %reduce_window_sum.23, pred[768,768]{1,0:T(8,128)(4,1)S(1)} %iota_compare_fusion, f32[2,2,768]{2,1,0:T(2,128)S(1)} %get-tuple-element.203), kind=kOutput, calls=%fused_computation.27 | convolution fusion | flops 3631349760 | bytes 3760128 | tf_op jit(solution)/shard_map/vljk,vlki->vlji/dot_general | solution.py:84
  144.9 1.4 copy.63
  146.3 45.4 %all_to_all.36 = f32[2,2,768,128]{3,1,0,2:T(2,128)S(1)} all-to-all(f32[2,2,768,128]{3,1,0,2:T(2,128)S(1)} %copy.63), channel_id=1, replica_groups=mesh['lon'=16,'lat'=32] {'lat'}, dimensions={2} | all-to-all | bytes 3145728 | tf_op jit(solution)/shard_map/all_to_all | solution.py:86
  191.7 0.9 copy.64
  192.6 1.5 convolution_bitcast_fusion
  194.1 2.1 %copy.66 = f32[2,64,24,128]{3,2,1,0:T(8,128)} copy(f32[2,64,24,128]{3,1,2,0:T(8,128)S(1)} %convolution_bitcast_fusion) | data formatting | bytes 3145728 | tf_op jit(solution)/shard_map/vlk,vlab->vkab/dot_general | solution.py:87
  (33 shorter events, 11.8 us)
Async XLA Ops:
  0.0 192.6 %copy-start = (f32[2,64,64]{2,1,0:T(8,128)S(1)}, f32[2,64,64]{2,1,0:T(8,128)}, u32[]{:S(2)}) copy-start(f32[2,64,64]{2,1,0:T(8,128)} %param.11) | copy-start | bytes 98308
  0.0 2.6 %copy-start.1 = (f32[24,128]{1,0:T(8,128)S(1)}, f32[24,128]{1,0:T(8,128)}, u32[]{:S(2)}) copy-start(f32[24,128]{1,0:T(8,128)} %param.9) | copy-start | bytes 36868
  85.5 49.1 %all-to-all-start = ((f32[2,64,24,128]{3,2,0,1:T(8,128)}), f32[2,64,24,128]{3,2,0,1:T(8,128)S(1)}, u32[]{:S(2)}, u32[]{:S(2)}) async-start(f32[2,64,24,128]{3,2,0,1:T(8,128)} %copy.61), calls=%async_computation | async-start | bytes 3145728 | tf_op jit(solution)/shard_map/all_to_all | solution.py:79
